TPU v7x, 32 devices: a whole 2x2x4 slice. The times are simulated.
32 devices in a mesh: ctx: 16 (over z, y, x), kvh: 2 (over core).
Axes of the slice: x: 2, y: 2, z: 4, core: 2. Of those that a mesh axis runs over, the one named last changes fastest.
Arguments:
- doc_lengths: int32 [9], replicated, may hold values from 1 to 896, 4096 in all
- queries: bfloat16 [4096, 1024], P('ctx', 'kvh'), may hold values from -6 to 6
- keys: bfloat16 [4096, 256], P('ctx', 'kvh'), may hold values from -6 to 6
- values: bfloat16 [4096, 256], P('ctx', 'kvh'), may hold values from -12 to 12
- o_weight: bfloat16 [1024, 4096], P('kvh'), may hold values from -0.1875 to 0.1875
Outputs:
- projected: bfloat16 [4096, 4096], P(('ctx', 'kvh'))
Inputs may be any that keep to these rules, and one draw needn't show every extreme that they name: `doc_lengths`: the documents in sequence order; they sum to 4096.
All inputs are finite; a program needn't handle non-finite values.
Results may differ from a plain program's by a relative error of at most 0.018.
Values may be sent and summed in bfloat16 or wider, within the bound.
A program may use at most 64 MiB of HBM per device.

v0:
```python
import functools
import math

import jax
import jax.numpy as jnp
from jax import lax
from jax.experimental import pallas as pl
from jax.experimental.pallas import tpu as pltpu
from jax.sharding import PartitionSpec as P

HEAD_WIDTH = 128
REACH = 7
CHUNK = 4
TILE = 512
NEG_FILL = -1e30


def kernel(
    n_ctx, n_kvh, docs, q_hbm, k_hbm, v_hbm, w_hbm, o_ref,
    kv, q, w, att, sbuf, rbuf,
    local_sem, send_a, send_b, recv, rs_send, rs_recv,
):
    i = lax.axis_index("ctx")
    g = lax.axis_index("kvh")
    rows = q.shape[0]
    half = rows // 2
    heads = q.shape[1] // HEAD_WIDTH
    span = REACH + 1
    last = 2 * n_ctx - 1
    out_rows = rows // n_kvh
    tiles = w.shape[1] // TILE
    own_gap = last - 2 * i

    def own_copies():
        for x in range(2):
            for j, ref in enumerate((k_hbm, v_hbm)):
                yield pltpu.make_async_copy(
                    ref.at[pl.ds(x * half, half)], kv.at[x * span, j], local_sem.at[2 * x + j]
                )

    own = list(own_copies())
    for copy in own:
        copy.start()

    barrier = pltpu.get_barrier_semaphore()

    def greet(chip):
        pl.semaphore_signal(
            barrier, inc=1, device_id={"ctx": chip}, device_id_type=pl.DeviceIdType.MESH
        )

    for d in range(1, REACH + 1):

        @pl.when(i >= d)
        def _():
            greet(i - d)

        @pl.when(i + d < n_ctx)
        def _():
            greet(i + d)

        @pl.when((i + d >= n_ctx) & (own_gap != d))
        def _():
            greet(last - i - d)

    for j in range(1, n_kvh):
        pl.semaphore_signal(
            barrier,
            inc=1,
            device_id={"kvh": lax.rem(g + j, n_kvh)},
            device_id_type=pl.DeviceIdType.MESH,
        )

    q_copy = pltpu.make_async_copy(q_hbm, q, local_sem.at[4])
    w_copy = pltpu.make_async_copy(w_hbm, w, local_sem.at[5])
    q_copy.start()
    for d in range(1, REACH + 1):

        @pl.when(i < d)
        def _():
            kv[d] = jnp.zeros(kv.shape[1:], kv.dtype)

    for copy in own:
        copy.wait()
    for d in range(1, REACH + 1):

        @pl.when(own_gap == d)
        def _():
            kv[span + d] = kv[0]

    selfs = jnp.where(own_gap <= REACH, 1, 0)
    pl.semaphore_wait(barrier, REACH - selfs + jnp.minimum(i, REACH) + n_kvh - 1)

    def send(x, slot, chip, sem):
        return pltpu.make_async_remote_copy(
            src_ref=kv.at[x * span],
            dst_ref=kv.at[slot],
            send_sem=sem,
            recv_sem=recv.at[slot],
            device_id={"ctx": chip},
            device_id_type=pl.DeviceIdType.MESH,
        )

    def each_send(act):
        for d in range(1, REACH + 1):

            @pl.when(i + d < n_ctx)
            def _():
                act(send(0, d, i + d, send_a.at[d]))

            @pl.when((i + d >= n_ctx) & (own_gap != d))
            def _():
                act(send(0, span + d, last - i - d, send_a.at[d]))

            @pl.when(i >= d)
            def _():
                act(send(1, span + d, i - d, send_b.at[d]))

    each_send(lambda copy: copy.start())
    w_copy.start()

    scale = math.log2(math.e) / math.sqrt(HEAD_WIDTH)
    q_copy.wait()

    def attend(x):
        stretch = x * last + (1 - 2 * x) * i
        base = pl.multiple_of(x * half, half)
        here = stretch * half + lax.broadcasted_iota(jnp.int32, (half, 1), 0)
        start = jnp.zeros((half, 1), jnp.int32)
        end = jnp.int32(0)
        for n in range(docs.shape[0]):
            end = end + docs[n]
            start = jnp.maximum(start, jnp.where(end <= here, end, 0))
        state = [None] * heads
        for first in range(0, span, CHUNK):
            for d in range(max(first, 1), first + CHUNK):

                @pl.when(((x == 0) & (i >= d)) | ((x == 1) & (own_gap != d)))
                def _():
                    slot = x * span + d
                    pltpu.make_async_copy(kv.at[slot], kv.at[slot], recv.at[slot]).wait()

            part = kv[pl.ds(x * span + first, CHUNK)]
            k = part[:, 0].reshape(CHUNK * half, HEAD_WIDTH)
            v = part[:, 1].reshape(CHUNK * half, HEAD_WIDTH)
            column = lax.broadcasted_iota(jnp.int32, (half, CHUNK * half), 1)
            there = (stretch - first) * half + column - 2 * half * (column // half)
            bias = jnp.where((there >= start) & (there <= here), 0.0, NEG_FILL)
            for h in range(heads):
                lanes = slice(h * HEAD_WIDTH, (h + 1) * HEAD_WIDTH)
                score = (
                    lax.dot_general(
                        q[pl.ds(base, half), lanes],
                        k,
                        (((1,), (1,)), ((), ())),
                        preferred_element_type=jnp.float32,
                    )
                    + bias
                )
                top = jnp.max(score, axis=1, keepdims=True)
                if first:
                    top = jnp.maximum(top, state[h][0])
                weight = jnp.exp2((score - top) * scale)
                total = jnp.sum(weight, axis=1, keepdims=True)
                out = jnp.dot(weight.astype(jnp.bfloat16), v, preferred_element_type=jnp.float32)
                if first:
                    factor = jnp.exp2((state[h][0] - top) * scale)
                    total = total + state[h][1] * factor
                    out = out + state[h][2] * factor
                state[h] = (top, total, out)
        for h in range(heads):
            lanes = slice(h * HEAD_WIDTH, (h + 1) * HEAD_WIDTH)
            att[pl.ds(base, half), lanes] = (state[h][2] / state[h][1]).astype(att.dtype)

    def project(p, t):
        return jnp.dot(
            att[pl.ds(pl.multiple_of(p * out_rows, out_rows), out_rows), :],
            w[:, t * TILE : (t + 1) * TILE],
            preferred_element_type=jnp.float32,
        )

    def hand_over(j, t):
        return pltpu.make_async_remote_copy(
            src_ref=sbuf.at[j - 1, t],
            dst_ref=rbuf.at[j - 1, t],
            send_sem=rs_send.at[j - 1, t],
            recv_sem=rs_recv.at[j - 1, t],
            device_id={"kvh": lax.rem(g + j, n_kvh)},
            device_id_type=pl.DeviceIdType.MESH,
        )

    def give():
        for j in range(1, n_kvh):
            for t in range(tiles):
                sbuf[j - 1, t] = project(lax.rem(g + j, n_kvh), t).astype(sbuf.dtype)
                hand_over(j, t).start()

    if n_kvh == 2:
        attend(1 - g)
        w_copy.wait()
        give()
        attend(g)
    else:
        attend(0)
        attend(1)
        w_copy.wait()
        give()
    for t in range(tiles):
        total = project(g, t)
        for j in range(1, n_kvh):
            hand_over(j, t).wait_recv()
            total = total + rbuf[j - 1, t].astype(jnp.float32)
        o_ref[:, t * TILE : (t + 1) * TILE] = total.astype(o_ref.dtype)
    each_send(lambda copy: copy.wait_send())
    for j in range(1, n_kvh):
        for t in range(tiles):
            hand_over(j, t).wait_send()


def local(n_ctx, n_kvh, doc_lengths, queries, keys, values, o_weight):
    rows, width = queries.shape
    half = rows // 2
    columns = o_weight.shape[1]
    out_rows = rows // n_kvh
    tiles = columns // TILE
    span = REACH + 1
    dtype = queries.dtype
    any_spec = pl.BlockSpec(memory_space=pl.ANY)
    return pl.pallas_call(
        functools.partial(kernel, n_ctx, n_kvh),
        out_shape=jax.ShapeDtypeStruct((out_rows, columns), dtype),
        in_specs=[pl.BlockSpec(memory_space=pltpu.SMEM)] + [any_spec] * 4,
        out_specs=pl.BlockSpec(memory_space=pltpu.VMEM),
        scratch_shapes=[
            pltpu.VMEM((2 * span, 2, half, HEAD_WIDTH), dtype),
            pltpu.VMEM((rows, width), dtype),
            pltpu.VMEM(o_weight.shape, dtype),
            pltpu.VMEM((rows, width), dtype),
            pltpu.VMEM((n_kvh - 1, tiles, out_rows, TILE), dtype),
            pltpu.VMEM((n_kvh - 1, tiles, out_rows, TILE), dtype),
            pltpu.SemaphoreType.DMA((6,)),
            pltpu.SemaphoreType.DMA((span,)),
            pltpu.SemaphoreType.DMA((span,)),
            pltpu.SemaphoreType.DMA((2 * span,)),
            pltpu.SemaphoreType.DMA((n_kvh - 1, tiles)),
            pltpu.SemaphoreType.DMA((n_kvh - 1, tiles)),
        ],
        compiler_params=pltpu.CompilerParams(
            collective_id=0, has_side_effects=True, vmem_limit_bytes=60 * 2**20
        ),
    )(doc_lengths, queries, keys, values, o_weight)


def solution(mesh):
    in_specs = (P(), P("ctx", "kvh"), P("ctx", "kvh"), P("ctx", "kvh"), P("kvh", None))
    out_specs = P(("ctx", "kvh"), None)
    return jax.shard_map(
        functools.partial(local, mesh.shape["ctx"], mesh.shape["kvh"]),
        mesh=mesh,
        in_specs=in_specs,
        out_specs=out_specs,
        check_vma=False,
    )
```

profile of v0, /device:TPU:2, one launch (start us, length us, event | category | flops | bytes accessed | tf_op | source)
XLA Modules:
  0.0 32.9 jit_solution(10851229103674175480)
XLA Ops:
  0.0 30.6 %shard_map.55 = bf16[128,4096]{1,0:T(8,128)(2,1)} custom-call(s32[9]{0:T(128)} %docs.1, bf16[256,512]{1,0:T(8,128)(2,1)} %q_hbm.1, bf16[256,128]{1,0:T(8,128)(2,1)} %k_hbm.1, bf16[256,128]{1,0:T(8,128)(2,1)} %v_hbm.1, bf16[512,4096]{1,0:T(8,128)(2,1)} %w_hbm.1), custom_call_target="tpu_custom_call" | custom-call | tf_op jit(solution)/shard_map/pallas_call | solution.py:229
  30.6 2.3 %copy.7 = bf16[128,4096]{1,0:T(8,128)(2,1)} copy(bf16[128,4096]{1,0:T(8,128)(2,1)} %shard_map.55) | data formatting | bytes 2097152
where the time goes:
time: 33 us; the launch traced here: 32.9 us
  Pallas kernels  30.6 us (93%)
  local copies, waits for them, and re-layouts  2.29 us (7%)
    pallas_call x1, Pallas kernels, local(): pl.pallas_call(functools.partial(kernel, n_ctx, n_kvh), out_shape=jax.Sha...  30.6 us
    unnamed x1, local copies, waits for them, and re-layouts  2.29 us

commit v1 on v0

v1 whole, which is shorter than its diff:
```python
import functools
import math

import jax
import jax.numpy as jnp
from jax import lax
from jax.experimental import pallas as pl
from jax.experimental.pallas import tpu as pltpu
from jax.sharding import PartitionSpec as P

HEAD_WIDTH = 128
GROUP = 4
CHUNK = 4
TILE = 512
NEG_FILL = -1e30


def kernel(
    n_ctx, n_kvh, docs, q_hbm, k_hbm, v_hbm, w_hbm, o_ref,
    kv, q, w, att, sbuf, rbuf,
    local_sem, send_sem, recv, rs_send, rs_recv,
):
    i = lax.axis_index("ctx")
    g = lax.axis_index("kvh")
    rows = q.shape[0]
    half = rows // 2
    heads = q.shape[1] // HEAD_WIDTH
    last = 2 * n_ctx - 1
    groups = n_ctx // GROUP
    p = i // GROUP
    b = i % GROUP
    peers = (b + 1 - 2 * (b % 2), (b + 2) % GROUP, 3 - b)
    has_above = p < groups - 1
    has_below = p > 0
    out_rows = rows // n_kvh
    tiles = w.shape[1] // TILE

    def own_copies():
        for x in range(2):
            for j, ref in enumerate((k_hbm, v_hbm)):
                yield pltpu.make_async_copy(
                    ref.at[pl.ds(x * half, half)], kv.at[8 + 4 * x + b, j], local_sem.at[2 * x + j]
                )

    own = list(own_copies())
    for copy in own:
        copy.start()

    barrier = pltpu.get_barrier_semaphore()

    def greet(**device):
        pl.semaphore_signal(
            barrier, inc=1, device_id=device, device_id_type=pl.DeviceIdType.MESH
        )

    @pl.when(has_above)
    def _():
        greet(ctx=i + GROUP)

    @pl.when(has_below)
    def _():
        greet(ctx=i - GROUP)

    for c in peers[:2]:
        greet(ctx=p * GROUP + c)
    for j in range(1, n_kvh):
        greet(kvh=lax.rem(g + j, n_kvh))

    q_copy = pltpu.make_async_copy(q_hbm, q, local_sem.at[4])
    w_copy = pltpu.make_async_copy(w_hbm, w, local_sem.at[5])
    q_copy.start()

    @pl.when(p < 2)
    def _():
        kv[0:4] = jnp.zeros((4, *kv.shape[1:]), kv.dtype)

    @pl.when(p < 1)
    def _():
        kv[4:8] = jnp.zeros((4, *kv.shape[1:]), kv.dtype)

    for copy in own:
        copy.wait()
    ends = jnp.where(has_above, 1, 0) + jnp.where(has_below, 1, 0)
    pl.semaphore_wait(barrier, 2 + ends + n_kvh - 1)

    def send(source, slot, chip, sem):
        return pltpu.make_async_remote_copy(
            src_ref=kv.at[source],
            dst_ref=kv.at[slot],
            send_sem=send_sem.at[sem],
            recv_sem=recv.at[slot],
            device_id={"ctx": chip},
            device_id_type=pl.DeviceIdType.MESH,
        )

    def arrive(slot):
        pltpu.make_async_copy(kv.at[slot], kv.at[slot], recv.at[slot]).wait()

    def up(c, sem, act):
        @pl.when(has_above)
        def _():
            act(send(8 + c, 4 + c, i + GROUP, sem))

    def down(c, sem, act):
        @pl.when(has_below)
        def _():
            act(send(12 + c, 16 + c, i - GROUP, sem))

    def up_again(c, act):
        @pl.when(has_above & has_below & (c > b))
        def _():
            act(send(4 + c, c, i + GROUP, 14 + c))

    def down_again(c, act):
        @pl.when(has_below & (c < b))
        def _():
            act(send(16 + c, 20 + c, i - GROUP, 18 + c))

    def give_own(k, act):
        act(send(8 + b, 8 + b, p * GROUP + peers[k], 2 * k))
        act(send(12 + b, 12 + b, p * GROUP + peers[k], 2 * k + 1))

    def pass_on(act):
        act(send(8 + peers[0], 8 + peers[0], p * GROUP + peers[1], 4))
        act(send(12 + peers[1], 12 + peers[1], p * GROUP + peers[0], 5))

    def start(copy):
        copy.start()

    up(b, 6, start)
    down(b, 7, start)
    give_own(0, start)
    give_own(1, start)
    w_copy.start()
    cx, cy, cd = peers
    arrive(8 + cx)
    up(cx, 8, start)
    arrive(12 + cy)
    pass_on(start)
    down(cy, 12, start)
    arrive(8 + cy)
    up(cy, 9, start)
    arrive(12 + cx)
    down(cx, 11, start)
    arrive(8 + cd)
    up(cd, 10, start)
    arrive(12 + cd)
    down(cd, 13, start)

    @pl.when(p == groups - 1)
    def _():
        for c in range(4):
            kv[16 + c] = kv[11 - c]

    for c in (b, *peers):

        @pl.when(has_below)
        def _():
            arrive(4 + c)

        up_again(c, start)

        @pl.when(has_above)
        def _():
            arrive(16 + c)

        down_again(c, start)

    @pl.when(p == groups - 1)
    def _():
        for c in range(3):
            kv[20 + c] = kv[7 - c]

    def far_arrive():
        for c in range(GROUP):

            @pl.when((p >= 2) & (c > b))
            def _():
                arrive(c)

            @pl.when((p < groups - 1) & (c < b))
            def _():
                arrive(20 + c)

    scale = math.log2(math.e) / math.sqrt(HEAD_WIDTH)
    q_copy.wait()
    bounds = [jnp.int32(0)]
    for n in range(docs.shape[0]):
        bounds.append(bounds[-1] + docs[n])

    def attend(x, far, state):
        stretch = x * last + (1 - 2 * x) * i
        base = pl.multiple_of(x * half, half)
        here = stretch * half + lax.broadcasted_iota(jnp.int32, (half, 1), 0)
        start = jnp.zeros((half, 1), jnp.int32)
        for end in bounds[1:]:
            start = jnp.maximum(start, jnp.where(end <= here, end, 0))
        first = b + 5 - 4 * far + x * (7 + 8 * far)
        part = kv[pl.ds(first, CHUNK)]
        k = part[:, 0].reshape(CHUNK * half, HEAD_WIDTH)
        v = part[:, 1].reshape(CHUNK * half, HEAD_WIDTH)
        column = lax.broadcasted_iota(jnp.int32, (1, CHUNK * half), 1)
        block = column // half
        order = (1 - x) * (block - CHUNK + 1) - x * block - CHUNK * far
        there = (stretch + order) * half + column - half * block
        bias = jnp.where((there >= start) & (there <= here), 0.0, NEG_FILL)
        made = []
        for h in range(heads):
            lanes = slice(h * HEAD_WIDTH, (h + 1) * HEAD_WIDTH)
            score = (
                lax.dot_general(
                    q[pl.ds(base, half), lanes],
                    k,
                    (((1,), (1,)), ((), ())),
                    preferred_element_type=jnp.float32,
                )
                + bias
            )
            top = jnp.max(score, axis=1, keepdims=True)
            if far:
                top = jnp.maximum(top, state[h][0])
            weight = jnp.exp2((score - top) * scale)
            total = jnp.sum(weight, axis=1, keepdims=True)
            out = jnp.dot(weight.astype(jnp.bfloat16), v, preferred_element_type=jnp.float32)
            if far:
                factor = jnp.exp2((state[h][0] - top) * scale)
                total = total + state[h][1] * factor
                out = out + state[h][2] * factor
                att[pl.ds(base, half), lanes] = (out / total).astype(att.dtype)
            made.append((top, total, out))
        return made

    def project(part, t):
        return jnp.dot(
            att[pl.ds(pl.multiple_of(part * out_rows, out_rows), out_rows), :],
            w[:, t * TILE : (t + 1) * TILE],
            preferred_element_type=jnp.float32,
        )

    def hand_over(j, t):
        return pltpu.make_async_remote_copy(
            src_ref=sbuf.at[j - 1, t],
            dst_ref=rbuf.at[j - 1, t],
            send_sem=rs_send.at[j - 1, t],
            recv_sem=rs_recv.at[j - 1, t],
            device_id={"kvh": lax.rem(g + j, n_kvh)},
            device_id_type=pl.DeviceIdType.MESH,
        )

    def give():
        for j in range(1, n_kvh):
            for t in range(tiles):
                sbuf[j - 1, t] = project(lax.rem(g + j, n_kvh), t).astype(sbuf.dtype)
                hand_over(j, t).start()

    split = n_kvh == 2
    sides = (1 - g, g) if split else (0, 1)
    near = [attend(x, 0, None) for x in sides]
    far_arrive()
    attend(sides[0], 1, near[0])
    if split:
        w_copy.wait()
        give()
        attend(sides[1], 1, near[1])
    else:
        attend(sides[1], 1, near[1])
        w_copy.wait()
        give()
    for t in range(tiles):
        total = project(g, t)
        for j in range(1, n_kvh):
            hand_over(j, t).wait_recv()
            total = total + rbuf[j - 1, t].astype(jnp.float32)
        o_ref[:, t * TILE : (t + 1) * TILE] = total.astype(o_ref.dtype)

    def sent(copy):
        copy.wait_send()

    up(b, 6, sent)
    down(b, 7, sent)
    give_own(0, sent)
    give_own(1, sent)
    pass_on(sent)
    for k, c in enumerate(peers):
        up(c, 8 + k, sent)
        down(c, 11 + k, sent)
    for c in (b, *peers):
        up_again(c, sent)
        down_again(c, sent)
    for j in range(1, n_kvh):
        for t in range(tiles):
            hand_over(j, t).wait_send()


def local(n_ctx, n_kvh, doc_lengths, queries, keys, values, o_weight):
    rows, width = queries.shape
    half = rows // 2
    columns = o_weight.shape[1]
    out_rows = rows // n_kvh
    tiles = columns // TILE
    dtype = queries.dtype
    any_spec = pl.BlockSpec(memory_space=pl.ANY)
    return pl.pallas_call(
        functools.partial(kernel, n_ctx, n_kvh),
        out_shape=jax.ShapeDtypeStruct((out_rows, columns), dtype),
        in_specs=[pl.BlockSpec(memory_space=pltpu.SMEM)] + [any_spec] * 4,
        out_specs=pl.BlockSpec(memory_space=pltpu.VMEM),
        scratch_shapes=[
            pltpu.VMEM((6 * GROUP, 2, half, HEAD_WIDTH), dtype),
            pltpu.VMEM((rows, width), dtype),
            pltpu.VMEM(o_weight.shape, dtype),
            pltpu.VMEM((rows, width), dtype),
            pltpu.VMEM((n_kvh - 1, tiles, out_rows, TILE), dtype),
            pltpu.VMEM((n_kvh - 1, tiles, out_rows, TILE), dtype),
            pltpu.SemaphoreType.DMA((6,)),
            pltpu.SemaphoreType.DMA((22,)),
            pltpu.SemaphoreType.DMA((6 * GROUP,)),
            pltpu.SemaphoreType.DMA((n_kvh - 1, tiles)),
            pltpu.SemaphoreType.DMA((n_kvh - 1, tiles)),
        ],
        compiler_params=pltpu.CompilerParams(
            collective_id=0, has_side_effects=True, vmem_limit_bytes=60 * 2**20
        ),
    )(doc_lengths, queries, keys, values, o_weight)

def solution(mesh):
    in_specs = (P(), P("ctx", "kvh"), P("ctx", "kvh"), P("ctx", "kvh"), P("kvh", None))
    out_specs = P(("ctx", "kvh"), None)
    return jax.shard_map(
        functools.partial(local, mesh.shape["ctx"], mesh.shape["kvh"]),
        mesh=mesh,
        in_specs=in_specs,
        out_specs=out_specs,
        check_vma=False,
    )
```

time: 33 us -> 28.8 us (0.87)
  the two profiles are of different devices: /device:TPU:2 before, /device:TPU:0 now
where the time goes in v1:
time: 28.8 us; the launch traced here: 28.6 us
  Pallas kernels  26.3 us (91%)
  local copies, waits for them, and re-layouts  2.29 us (8%)
    pallas_call x1, Pallas kernels, local(): pl.pallas_call(functools.partial(kernel, n_ctx, n_kvh), out_shape=jax.Sha...  26.3 us
    unnamed x1, local copies, waits for them, and re-layouts  2.29 us

profile of v1, /device:TPU:0, one launch (start us, length us, event | category | flops | bytes accessed | tf_op | source)
XLA Modules:
  0.0 28.6 jit_solution(14708647122104518969)
XLA Ops:
  0.0 26.3 %shard_map.55 = bf16[128,4096]{1,0:T(8,128)(2,1)} custom-call(s32[9]{0:T(128)} %docs.1, bf16[256,512]{1,0:T(8,128)(2,1)} %q_hbm.1, bf16[256,128]{1,0:T(8,128)(2,1)} %k_hbm.1, bf16[256,128]{1,0:T(8,128)(2,1)} %v_hbm.1, bf16[512,4096]{1,0:T(8,128)(2,1)} %w_hbm.1), custom_call_target="tpu_custom_call" | custom-call | tf_op jit(solution)/shard_map/pallas_call | solution.py:303
  26.3 2.3 %copy.7 = bf16[128,4096]{1,0:T(8,128)(2,1)} copy(bf16[128,4096]{1,0:T(8,128)(2,1)} %shard_map.55) | data formatting | bytes 2097152
